TPU v7x, 32 devices: a whole 2x2x4 slice. The times are simulated.
32 devices in a mesh: req: 4 (over z), cand: 8 (over y, x, core).
Axes of the slice: x: 2, y: 2, z: 4, core: 2. Of those that a mesh axis runs over, the one named last changes fastest.
Arguments:
- dense_feat: bfloat16 [4096, 896], P(('req', 'cand')), may hold values from -6 to 6
- emb_ids: int32 [8, 4, 4096], P('cand', None, 'req'), may hold values from 0 to 32767
- tables: bfloat16 [8, 16, 32768], P('cand'), may hold values from -3 to 3
- history_kv: bfloat16 [8, 64, 2048], P('req', 'cand'), may hold values from -6 to 6
- hist_len: int32 [8], P('req'), may hold values from 1 to 64, 256 in all
- cand_request: int32 [4096], P(('req', 'cand')), may hold values from 0 to 1
- w_query: bfloat16 [1024, 1024], P(('req', 'cand')), may hold values from -0.1875 to 0.1875
- w_out: bfloat16 [1024, 1024], P(('req', 'cand')), may hold values from -0.1875 to 0.1875
- cotangent: bfloat16 [4096, 1024], P(('req', 'cand')), may hold values from -2 to 2
Outputs:
- cand_out: bfloat16 [4096, 1024], P(('req', 'cand'))
- d_kv: float32 [8, 64, 2048], P('req', 'cand')
- d_pooled: bfloat16 [8, 16, 4096], P('cand', None, 'req')
Inputs may be any that keep to these rules, and one draw needn't show every extreme that they name: `hist_len`: the lengths sum to 256 and the largest equals 64.
All inputs are finite; a program needn't handle non-finite values. No bound on the sum of `hist_len` on one device may be relied on, other than what follows from the above.
Results may differ from a plain program's by a relative error of at most 0.023.
Values may be sent and summed in bfloat16 or wider, within the bound.
A program may use at most 64 MiB of HBM per device.

v0:
```python
import math

import jax
import jax.numpy as jnp
from jax import lax
from jax.sharding import PartitionSpec as P

H = 8


norm_eps = 1e-05


def silu_slope(argument):
    sigmoid_value = jax.nn.sigmoid(argument)
    return sigmoid_value * (1.0 + argument * (1.0 - sigmoid_value))


def event_mask(requests, lengths, row_count):
    owned_count = lengths.shape[0]
    positions = jnp.arange(row_count, dtype=jnp.int32)
    in_length = positions[None, :] < lengths[:, None]
    same_request = requests[:, None] == jnp.arange(owned_count, dtype=jnp.int32)[None, :]
    joined_mask = same_request[:, :, None] & in_length[None, :, :]
    return joined_mask.reshape(requests.shape[0], owned_count * row_count).astype(jnp.float32)


def forward_events(query_heads, kv_piece, live_mask, score_scale):
    owned_count, row_count, kv_width = kv_piece.shape
    model_width = kv_width // 2
    events = owned_count * row_count
    flat_events = kv_piece.reshape(events, kv_width)
    key_heads = flat_events[:, :model_width].reshape(events, H, model_width // H)
    value_heads = flat_events[:, model_width:].reshape(events, H, model_width // H)
    scores = (
        jnp.einsum("chd,ehd->che", query_heads, key_heads, preferred_element_type=jnp.float32)
        * score_scale
    )
    weights = (jax.nn.silu(scores) * live_mask[:, None, :]).astype(jnp.bfloat16)
    return (scores, weights, key_heads, value_heads)


def backward_core(
    query_heads, back_att, scores, weights, key_heads, value_heads, live_mask, score_scale
):
    back_w = jnp.einsum("chd,ehd->che", back_att, value_heads, preferred_element_type=jnp.float32)
    back_s = (back_w * live_mask[:, None, :] * silu_slope(scores) * score_scale).astype(
        jnp.bfloat16
    )
    back_query = jnp.einsum("che,ehd->chd", back_s, key_heads, preferred_element_type=jnp.float32)
    key_part = jnp.einsum("che,chd->ehd", back_s, query_heads, preferred_element_type=jnp.float32)
    value_part = jnp.einsum("che,chd->ehd", weights, back_att, preferred_element_type=jnp.float32)
    events = key_part.shape[0]
    joined = jnp.concatenate([key_part.reshape(events, -1), value_part.reshape(events, -1)], axis=1)
    return (back_query, joined.astype(jnp.bfloat16))


def take_columns(table, indices):
    return jnp.take(table, indices, axis=1)


def on_device(
    dense_feat, emb_ids, tables, history_kv, hist_len, cand_request, w_query, w_out, cotangent
):
    tab_dev, emb_width, table_rows = tables.shape
    bag_size = emb_ids.shape[1]
    group_size = emb_ids.shape[2]
    pooled_sum = jnp.zeros((tab_dev, emb_width, group_size), jnp.float32)
    for slot in range(bag_size):
        pooled_sum = pooled_sum + jax.vmap(take_columns)(tables, emb_ids[:, slot, :]).astype(
            jnp.float32
        )
    pooled_rows = pooled_sum.astype(jnp.bfloat16).reshape(tab_dev * emb_width, group_size)
    pooled_cols = lax.all_to_all(pooled_rows, "cand", split_axis=1, concat_axis=0, tiled=True)
    pooled = jnp.transpose(pooled_cols, (1, 0))
    features = jnp.concatenate([pooled, dense_feat], axis=1)
    cand_count, model_width = features.shape
    pooled_width = pooled.shape[1]
    head_dim = model_width // H
    score_scale = 1.0 / math.sqrt(head_dim)
    owned_count, shard_events, kv_width = history_kv.shape
    hist_events = shard_events * lax.axis_size("cand")
    full_query, full_out = (
        lax.all_gather(w_query, ("req", "cand"), axis=0, tiled=True),
        lax.all_gather(w_out, ("req", "cand"), axis=0, tiled=True),
    )
    query_pre = jnp.dot(features, full_query, preferred_element_type=jnp.float32)
    query_heads = jax.nn.silu(query_pre).astype(jnp.bfloat16).reshape(cand_count, H, head_dim)
    full_history = lax.all_gather(history_kv, "cand", axis=1, tiled=True)
    live_mask = event_mask(cand_request, hist_len, hist_events)
    scores, weights, key_heads, value_heads = forward_events(
        query_heads, full_history, live_mask, score_scale
    )
    attended = jnp.einsum("che,ehd->chd", weights, value_heads, preferred_element_type=jnp.float32)
    attended = attended.reshape(cand_count, model_width)
    centered = attended - jnp.mean(attended, axis=1, keepdims=True)
    inverse = lax.rsqrt(jnp.mean(centered * centered, axis=1, keepdims=True) + norm_eps)
    normed = centered * inverse
    normed_b = normed.astype(jnp.bfloat16)
    mixed_out = jnp.dot(normed_b, full_out, preferred_element_type=jnp.float32)
    back_y = lax.dot_general(
        cotangent, full_out, (((1,), (1,)), ((), ())), preferred_element_type=jnp.float32
    )
    cand_out = (mixed_out + features.astype(jnp.float32)).astype(jnp.bfloat16)
    back_att = inverse * (
        back_y
        - jnp.mean(back_y, axis=1, keepdims=True)
        - normed * jnp.mean(back_y * normed, axis=1, keepdims=True)
    )
    back_att = back_att.astype(jnp.bfloat16).reshape(cand_count, H, head_dim)
    back_query, joined = backward_core(
        query_heads, back_att, scores, weights, key_heads, value_heads, live_mask, score_scale
    )
    kv_part = joined.reshape(owned_count, hist_events, kv_width)
    d_kv = lax.psum_scatter(kv_part, "cand", scatter_dimension=1, tiled=True).astype(jnp.float32)
    back_pre = (back_query.reshape(cand_count, model_width) * silu_slope(query_pre)).astype(
        jnp.bfloat16
    )
    back_columns = lax.dot_general(
        back_pre,
        full_query[:pooled_width],
        (((1,), (1,)), ((), ())),
        preferred_element_type=jnp.float32,
    )
    back_pool = (cotangent[:, :pooled_width].astype(jnp.float32) + back_columns).astype(
        jnp.bfloat16
    )
    pool_cols = jnp.transpose(back_pool, (1, 0))
    pool_rows = lax.all_to_all(pool_cols, "cand", split_axis=0, concat_axis=1, tiled=True)
    d_pooled = pool_rows.reshape(tab_dev, emb_width, pool_rows.shape[1])
    return (cand_out, d_kv, d_pooled)


def solution(mesh):
    return jax.shard_map(
        on_device,
        mesh=mesh,
        in_specs=(
            P(("req", "cand"), None),
            P("cand", None, "req"),
            P("cand", None, None),
            P("req", "cand", None),
            P("req"),
            P(("req", "cand")),
            P(("req", "cand"), None),
            P(("req", "cand"), None),
            P(("req", "cand"), None),
        ),
        out_specs=(P(("req", "cand"), None), P("req", "cand", None), P("cand", None, "req")),
        check_vma=False,
    )
```

profile of v0, /device:TPU:0, one launch (start us, length us, event | category | flops | bytes accessed | tf_op | source)
XLA Modules:
  0.0 175.3 jit_solution(15965709594702784721)
XLA Ops:
  7.2 0.0 all-gather.3.cloned.1.call-start
  7.2 0.7 all-gather.3.cloned.1.call-update
  7.9 0.0 all-gather.5.cloned.1.call-start
  7.9 0.7 all-gather.5.cloned.1.call-update
  8.7 7.1 %copy.95 = bf16[1,16,32768]{1,2,0:T(8,128)(2,1)} copy(bf16[1,16,32768]{2,1,0:T(8,128)(2,1)} %param.13) | data formatting | bytes 2097152 | tf_op args[2]
  15.7 0.1 and_reduce_fusion.3
  15.9 11.8 %gather_fusion.2 = bf16[1024,16]{1,0:T(8,128)(2,1)S(1)} fusion(bf16[1,16,32768]{1,2,0:T(8,128)(2,1)} %copy.95, s32[1024]{0:T(1024)S(1)} %bitcast.121), kind=kCustom, calls=%fused_computation.2.clone | custom fusion | bytes 73728 | tf_op jit(solution)/shard_map/vmap(jit(_take))/gather | solution.py:59
  27.7 0.0 copy-start.4
  27.7 0.1 copy.100
  27.9 11.8 %gather_fusion.3 = bf16[1024,16]{1,0:T(8,128)(2,1)S(1)} fusion(bf16[1,16,32768]{1,2,0:T(8,128)(2,1)} %copy.95, s32[1024]{0:T(1024)S(1)} %bitcast.122), kind=kCustom, calls=%fused_computation.3.clone | custom fusion | bytes 73728 | tf_op jit(solution)/shard_map/vmap(jit(_take))/gather | solution.py:59
  39.6 0.1 copy.102
  39.8 0.0 copy-start.6
  39.8 11.9 %gather_fusion = bf16[1024,16]{1,0:T(8,128)(2,1)S(1)} fusion(bf16[1,16,32768]{1,2,0:T(8,128)(2,1)} %copy.95, s32[1024]{0:T(1024)S(1)} %bitcast.123), kind=kCustom, calls=%fused_computation.clone | custom fusion | bytes 73728 | tf_op jit(solution)/shard_map/vmap(jit(_take))/gather | solution.py:59
  51.7 0.0 copy-start.7
  51.7 0.1 copy.96
  51.9 0.0 slice-start
  51.9 0.0 copy-start.2
  51.9 12.3 %gather_fusion.1 = bf16[1024,16]{1,0:T(8,128)(2,1)S(1)} fusion(bf16[1,16,32768]{1,2,0:T(8,128)(2,1)} %copy.95, s32[1024]{0:T(1024)S(1)} %bitcast.120), kind=kCustom, calls=%fused_computation.1.clone | custom fusion | bytes 73728 | tf_op jit(solution)/shard_map/vmap(jit(_take))/gather | solution.py:59
  64.2 0.1 copy.98
  64.4 0.6 copy.103
  65.0 5.5 %all-to-all-start = ((bf16[16,8,128]{2,0,1:T(8,128)(2,1)}), bf16[16,8,128]{2,0,1:T(8,128)(2,1)S(1)}, u32[]{:S(2)}, u32[]{:S(2)}) async-start(bf16[16,8,128]{2,0,1:T(8,128)(2,1)} %copy.103), calls=%async_computation | async-start | bytes 65536 | tf_op jit(solution)/shard_map/all_to_all | solution.py:74
  70.5 0.0 reduce-scatter.4.cloned.1.call-start
  70.5 10.3 %all_gather.10 = bf16[2,64,2048]{2,1,0:T(8,128)(2,1)S(1)} all-gather(bf16[2,8,2048]{2,1,0:T(8,128)(2,1)S(1)} %copy-done.4), channel_id=1, replica_groups=mesh['req'=4,'cand'=8] {'cand'}, dimensions={1}, use_global_device_ids=true | all-gather | bytes 589824 | tf_op jit(solution)/shard_map/all_gather | solution.py:89
  80.9 0.2 copy.105
  81.1 0.1 lt.28
  81.2 0.1 lt.29
  81.3 0.1 lt.30
  81.4 0.1 fusion.17
  81.4 0.1 copy.108
  81.5 0.2 copy.109
  81.7 0.1 copy.126
  81.9 0.1 copy.104
  82.0 0.0 all-gather.3.cloned.1.call-done
  82.0 2.8 %multiply_convert_fusion.3 = (bf16[128,1024]{1,0:T(8,128)(2,1)S(1)}, f32[128,1024]{1,0:T(8,128)}) fusion(bf16[1024,1024]{1,0:T(8,128)(2,1)} %all-gather.3.cloned.1.call-done, bf16[128,896]{1,0:T(8,128)(2,1)S(1)} %copy-done.2, bf16[128,128]{1,0:T(8,128)(2,1)S(1)} %bitcast.138), kind=kOutput, calls=%fused_computation.29 | convolution fusion | flops 269615104 | bytes 3145728 | tf_op jit(solution)/shard_map/dot_general | solution.py:87
  84.8 0.2 copy.127
  85.0 0.4 multiply_convert_fusion.2
  85.4 0.3 fusion.35
  85.8 0.2 copy.110
  86.0 0.2 fusion.10
  86.1 42.0 %all-gather.5.cloned.1.call-done = bf16[1024,1024]{1,0:T(8,128)(2,1)} async-done(((bf16[32,1024]{1,0:T(8,128)(2,1)}), bf16[1024,1024]{1,0:T(8,128)(2,1)}) %all-gather.5.cloned.1.call-update) | async-done | bytes 2097168 | tf_op jit(solution)/shard_map/all_gather | solution.py:85
  128.1 2.5 %fusion.33 = (f32[128]{0:T(128)S(1)}, f32[128]{0:T(128)S(1)}, f32[128,1024]{1,0:T(8,128)S(1)}) fusion(f32[128]{0:T(128)S(1)} %add_rsqrt_fusion, f32[128,1024]{1,0:T(8,128)S(1)} %copy.110, f32[128]{0:T(128)S(1)} %broadcast_multiply_fusion.2, bf16[128,1024]{1,0:T(8,128)(2,1)S(1)} %copy-done.1, bf16[1024,1024]{1,0:T(8,128)(2,1)} %all-gather.5.cloned.1.call-done), kind=kOutput, calls=%fused_computation.85 | convolution fusion | flops 269090560 | bytes 3409920 | tf_op jit(solution)/shard_map/dot_general | solution.py:101
  130.6 0.2 multiply_convert_fusion.1
  130.9 0.2 copy.128
  131.0 0.2 fusion.7
  131.3 0.4 fusion.4
  131.6 0.2 fusion.6
  131.9 0.2 copy.115
  132.1 0.1 concatenate.13
  132.2 0.2 copy.117
  132.4 0.1 concatenate.14
  132.5 0.5 copy.124
  133.1 1.0 copy.130
  134.0 0.0 reduce-scatter.4.cloned.1.call-update
  134.1 0.3 fusion.36
  134.4 0.0 copy-start.3
  134.4 1.0 copy.123
  135.4 2.3 %fusion.8 = bf16[128,128]{0,1:T(8,128)(2,1)} fusion(bf16[1024,1024]{1,0:T(8,128)(2,1)} %all-gather.3.cloned.1.call-done, f32[128,1024]{1,0:T(8,128)} %copy.123, f32[128,1024]{1,0:T(8,128)} %get-tuple-element.23, bf16[128,128]{0,1:T(8,128)(2,1)S(1)} %copy.126), kind=kOutput, calls=%fused_computation.18 | convolution fusion | flops 34783232 | bytes 1376256 | tf_op jit(solution)/shard_map/dot_general | solution.py:119
  137.7 3.3 %all-to-all-start.1 = ((bf16[8,16,128]{2,1,0:T(8,128)(2,1)}), bf16[8,16,128]{2,1,0:T(8,128)(2,1)S(1)}, u32[]{:S(2)}, u32[]{:S(2)}) async-start(bf16[8,16,128]{2,1,0:T(8,128)(2,1)} %bitcast.40), calls=%async_computation.1 | async-start | bytes 65536 | tf_op jit(solution)/shard_map/all_to_all | solution.py:129
  141.0 1.2 fusion.5
  142.2 3.6 %all-to-all-done.1 = bf16[8,16,128]{2,1,0:T(8,128)(2,1)S(1)} async-done(((bf16[8,16,128]{2,1,0:T(8,128)(2,1)}), bf16[8,16,128]{2,1,0:T(8,128)(2,1)S(1)}, u32[]{:S(2)}, u32[]{:S(2)}) %all-to-all-start.1) | async-done | bytes 32800 | tf_op jit(solution)/shard_map/all_to_all | solution.py:129
  145.8 0.6 reshape.181
  146.4 20.8 %reduce-scatter.4.cloned.1.call-done = bf16[8,4096]{1,0:T(8,128)(2,1)} async-done(((bf16[64,4096]{1,0:T(8,128)(2,1)}), bf16[8,4096]{1,0:T(8,128)(2,1)}) %reduce-scatter.4.cloned.1.call-update) | async-done | bytes 65552
  167.2 0.9 reshape.235
  168.1 0.7 copy_convert_fusion
  (32 shorter events, 0.3 us)
Async XLA Ops:
  7.2 74.8 %all-gather.3.cloned.1.call-start = ((), (), s32[]{:S(2)}) async-start(), calls=%async_computation.3 | async-start | bytes 2162688 | tf_op jit(solution)/shard_map/all_gather | solution.py:84
  7.9 120.2 %all-gather.5.cloned.1.call-start = ((), (), s32[]{:S(2)}) async-start(), calls=%async_computation.4 | async-start | bytes 2162688 | tf_op jit(solution)/shard_map/all_gather | solution.py:85
  8.6 7.1 %copy-start.5 = (s32[1,4,1024]{2,1,0:T(4,128)S(1)}, s32[1,4,1024]{2,1,0:T(4,128)}, u32[]{:S(2)}) copy-start(s32[1,4,1024]{2,1,0:T(4,128)} %param.12) | copy-start | bytes 49156
  27.7 42.8 %copy-start.4 = (bf16[2,8,2048]{2,1,0:T(8,128)(2,1)S(1)}, bf16[2,8,2048]{2,1,0:T(8,128)(2,1)}, u32[]{:S(2)}) copy-start(bf16[2,8,2048]{2,1,0:T(8,128)(2,1)} %param.14) | copy-start | bytes 196612
  39.8 41.1 %copy-start.6 = (s32[128]{0:T(128)S(1)}, s32[128]{0:T(128)}, u32[]{:S(2)}) copy-start(s32[128]{0:T(128)} %param.16) | copy-start | bytes 1540
  51.7 29.5 %copy-start.7 = (s32[2]{0:T(128)S(1)}, s32[2]{0:T(128)}, u32[]{:S(2)}) copy-start(s32[2]{0:T(128)} %param.15) | copy-start | bytes 28
  51.9 29.9 %slice-start = ((bf16[128,1024]{1,0:T(8,128)(2,1)}), bf16[128,128]{1,0:T(8,128)(2,1)S(1)}, s32[]{:S(2)}) async-start(bf16[128,1024]{1,0:T(8,128)(2,1)} %param.19), calls=%async_computation.6 | async-start | bytes 65536 | tf_op jit(solution)/shard_map/slice | solution.py:125
  51.9 30.1 %copy-start.2 = (bf16[128,896]{1,0:T(8,128)(2,1)S(1)}, bf16[128,896]{1,0:T(8,128)(2,1)}, u32[]{:S(2)}) copy-start(bf16[128,896]{1,0:T(8,128)(2,1)} %param.11) | copy-start | bytes 688132
  65.0 16.9 %all-to-all-start = ((bf16[16,8,128]{2,0,1:T(8,128)(2,1)}), bf16[16,8,128]{2,0,1:T(8,128)(2,1)S(1)}, u32[]{:S(2)}, u32[]{:S(2)}) async-start(bf16[16,8,128]{2,0,1:T(8,128)(2,1)} %copy.103), calls=%async_computation | async-start | bytes 65536 | tf_op jit(solution)/shard_map/all_to_all | solution.py:74
  70.5 96.7 %reduce-scatter.4.cloned.1.call-start = ((), (), s32[]{:S(2)}) async-start(), calls=%async_computation.5 | async-start | bytes 589824
  85.0 43.1 %copy-start.1 = (bf16[128,1024]{1,0:T(8,128)(2,1)S(1)}, bf16[128,1024]{1,0:T(8,128)(2,1)}, u32[]{:S(2)}) copy-start(bf16[128,1024]{1,0:T(8,128)(2,1)} %param.19) | copy-start | bytes 786436
  134.4 6.6 %copy-start = (bf16[1024,1024]{1,0:T(8,128)(2,1)S(1)}, bf16[1024,1024]{1,0:T(8,128)(2,1)}, u32[]{:S(2)}) copy-start(bf16[1024,1024]{1,0:T(8,128)(2,1)} %all-gather.5.cloned.1.call-done) | copy-start | bytes 6291460
  134.4 6.6 %copy-start.3 = (bf16[128,896]{1,0:T(8,128)(2,1)S(1)}, bf16[128,896]{1,0:T(8,128)(2,1)}, u32[]{:S(2)}) copy-start(bf16[128,896]{1,0:T(8,128)(2,1)} %param.11) | copy-start | bytes 688132
  137.7 8.1 %all-to-all-start.1 = ((bf16[8,16,128]{2,1,0:T(8,128)(2,1)}), bf16[8,16,128]{2,1,0:T(8,128)(2,1)S(1)}, u32[]{:S(2)}, u32[]{:S(2)}) async-start(bf16[8,16,128]{2,1,0:T(8,128)(2,1)} %bitcast.40), calls=%async_computation.1 | async-start | bytes 65536 | tf_op jit(solution)/shard_map/all_to_all | solution.py:129
Sparse Core Ops, SparseCore 0:
  10.9 59.0 all-gather.2
  72.8 55.2 all-gather.4
  134.2 32.9 reduce-scatter.3
where the time goes:
time: 176 us; the launch traced here: 175 us
  waiting for transfers between devices  67.7 us (38%)
  local copies, waits for them, and re-layouts  62.1 us (35%)
  between operations  14.2 us (8%)
  matrix products  10.6 us (6%)
  blocking collectives  10.3 us (6%)
  starting transfers between devices  8.95 us (5%)
    gather x12, local copies, waits for them, and re-layouts, take_columns(): return jnp.take(table, indices, axis=1)  48.2 us
    all_gather x1, waiting for transfers between devices, on_device(): lax.all_gather(w_out, ('req', 'cand'), axis=0, tiled=True)  42 us
    unnamed x4, waiting for transfers between devices  22.2 us
    all_gather x1, blocking collectives, on_device(): full_history = lax.all_gather(history_kv, 'cand', axis=1, tiled=True)  10.3 us
    unnamed x22, local copies, waits for them, and re-layouts  9.61 us
    all_to_all x1, starting transfers between devices, on_device(): lax.all_to_all(pooled_rows, 'cand', split_axis=1, concat_axis=0, tiled=True)  5.5 us
    all_to_all x1, waiting for transfers between devices, on_device(): lax.all_to_all(pool_cols, 'cand', split_axis=0, concat_axis=1, tiled=True)  3.55 us
  transfers between devices with their start and end apart: 5, of which 3 were waited for; matrix products, arithmetic and copies ran while one was open for 38% of the time, Pallas kernels for 0%

commit v1 on v0

--- a/solution.py
+++ b/solution.py
@@ -1,8 +1,11 @@
+import functools
 import math
 
 import jax
 import jax.numpy as jnp
 from jax import lax
+from jax.experimental import pallas as pl
+from jax.experimental.pallas import tpu as pltpu
 from jax.sharding import PartitionSpec as P
 
 H = 8
@@ -131,9 +134,416 @@
     return (cand_out, d_kv, d_pooled)
 
 
+MESH = pl.DeviceIdType.MESH
+LOOKUP_DEPTH = 512
+LOOKUP_WIDTH = 256
+
+
+def flip(index, bit):
+    return index + bit - 2 * bit * lax.rem(lax.div(index, bit), 2)
+
+
+def powers(count):
+    return [1 << k for k in reversed(range(count.bit_length() - 1))]
+
+
+class Gather:
+    def __init__(self, full, own, rounds, place, sends, recvs):
+        self.full, self.own, self.rounds, self.place = full, own, rounds, place
+        self.sends, self.recvs, self.rows = sends, recvs, own.shape[0]
+        self.count = 1 << len(rounds)
+
+    def device(self, subset):
+        req, cand = lax.axis_index("req"), lax.axis_index("cand")
+        for step, (axis, bit) in enumerate(self.rounds):
+            if subset >> step & 1:
+                if axis == "req":
+                    req = flip(req, bit)
+                else:
+                    cand = flip(cand, bit)
+        return req, cand
+
+    def block(self, subset):
+        first = pl.multiple_of(self.place(*self.device(subset)) * self.rows, self.rows)
+        return self.full.at[pl.ds(first, self.rows)]
+
+    def copy(self, subset, arrived):
+        step = subset.bit_length() - 1
+        sent = subset - (1 << step)
+        here = self.block(subset if arrived else sent)
+        return pltpu.make_async_remote_copy(
+            src_ref=self.own if sent == 0 and not arrived else here,
+            dst_ref=here,
+            send_sem=self.sends.at[subset],
+            recv_sem=self.recvs.at[subset],
+            device_id=self.device(1 << step),
+            device_id_type=MESH,
+        )
+
+    def forward(self, subset):
+        if subset:
+            self.copy(subset, True).wait_recv()
+        for step in range(subset.bit_length(), len(self.rounds)):
+            self.copy(subset + (1 << step), False).start()
+
+    def keep_own(self):
+        self.block(0)[...] = self.own[...]
+
+    def drain(self):
+        for subset in range(1, self.count):
+            self.copy(subset, False).wait_send()
+
+
+def dot_nt(left, right):
+    return lax.dot_general(
+        left, right, (((1,), (1,)), ((), ())), preferred_element_type=jnp.float32
+    )
+
+
+def dot_tn(left, right):
+    return lax.dot_general(
+        left, right, (((0,), (0,)), ((), ())), preferred_element_type=jnp.float32
+    )
+
+
+def dot_nn(left, right):
+    return jnp.dot(left, right, preferred_element_type=jnp.float32)
+
+
+def layer_kernel(
+    n_req,
+    n_cand,
+    lens_ref,
+    dense_ref,
+    ids_ref,
+    table_ref,
+    hist_ref,
+    requests_ref,
+    wq_ref,
+    wo_ref,
+    cot_ref,
+    out_ref,
+    dkv_ref,
+    dpool_ref,
+    wq,
+    wo,
+    hist,
+    lookup,
+    pool_acc,
+    pool_send,
+    pool_recv,
+    att,
+    query,
+    back_att,
+    scores_s,
+    weights_s,
+    back_query,
+    part,
+    part_recv,
+    grad_send,
+    grad_recv,
+    wq_sends,
+    wq_recvs,
+    wo_sends,
+    wo_recvs,
+    hist_sends,
+    hist_recvs,
+    pool_sends,
+    pool_recvs,
+    part_sends,
+    part_recvs,
+    grad_sends,
+    grad_recvs,
+):
+    req, cand = lax.axis_index("req"), lax.axis_index("cand")
+    cand_count, model_width = cot_ref.shape
+    emb_width = table_ref.shape[0]
+    head_dim = model_width // H
+    owned = lens_ref.shape[0]
+    block_events = hist_ref.shape[0]
+    events = block_events * n_cand
+    shard_events = block_events // owned
+    pooled_width = emb_width * n_cand
+    score_scale = 1.0 / math.sqrt(head_dim)
+
+    barrier = pltpu.get_barrier_semaphore()
+    greeted = [(flip(req, bit), cand) for bit in powers(n_req)]
+    greeted += [(req, lax.rem(cand + k, n_cand)) for k in range(1, n_cand)]
+    for device in greeted:
+        pl.semaphore_signal(barrier, inc=1, device_id=device, device_id_type=MESH)
+    pl.semaphore_wait(barrier, len(greeted))
+
+    req_rounds = [("req", bit) for bit in powers(n_req)]
+    cand_rounds = [("cand", bit) for bit in powers(n_cand)]
+    swapped = cand_rounds[:-1][::-1] + cand_rounds[-1:]
+
+    def linear(r, c):
+        return r * n_cand + c
+
+    def in_group(r, c):
+        return c
+
+    gq = Gather(wq, wq_ref, req_rounds + cand_rounds, linear, wq_sends, wq_recvs)
+    go = Gather(wo, wo_ref, req_rounds + swapped, linear, wo_sends, wo_recvs)
+    gh = Gather(hist, hist_ref, cand_rounds, in_group, hist_sends, hist_recvs)
+    gq.forward(0)
+    gh.forward(0)
+    go.forward(0)
+    for gather in (gq, gh, go):
+        gather.keep_own()
+
+    def exchange(source, target, sends, recvs, rows, k):
+        peer = lax.rem(cand + k, n_cand)
+        sent = pl.ds(pl.multiple_of(peer * rows, rows), rows)
+        mine = pl.ds(pl.multiple_of(cand * rows, rows), rows)
+        return pltpu.make_async_remote_copy(
+            src_ref=source.at[sent],
+            dst_ref=target.at[mine],
+            send_sem=sends.at[k],
+            recv_sem=recvs.at[k],
+            device_id=(req, peer),
+            device_id_type=MESH,
+        )
+
+    def start_all(*buffers):
+        for k in range(1, n_cand):
+            exchange(*buffers, k).start()
+
+    def own_rows(source, target, rows):
+        mine = pl.ds(pl.multiple_of(cand * rows, rows), rows)
+        target[mine] = source[mine]
+
+    def wait_all(*buffers):
+        for k in range(1, n_cand):
+            exchange(*buffers, k).wait()
+
+    highs = table_ref.shape[1] // LOOKUP_DEPTH
+    for high in range(highs):
+        lookup[high * emb_width : (high + 1) * emb_width, :] = table_ref[
+            :, high * LOOKUP_DEPTH : (high + 1) * LOOKUP_DEPTH
+        ]
+    pool_acc[...] = jnp.zeros_like(pool_acc)
+    chunks = ids_ref.shape[1] // LOOKUP_WIDTH
+    steps = chunks * ids_ref.shape[0]
+
+    def look_up(step, carry):
+        slot = lax.div(step, chunks)
+        columns = pl.ds(
+            pl.multiple_of(lax.rem(step, chunks) * LOOKUP_WIDTH, LOOKUP_WIDTH), LOOKUP_WIDTH
+        )
+        ids = ids_ref[pl.ds(slot, 1), columns]
+        low = ids & (LOOKUP_DEPTH - 1)
+        high_ids = ids >> (LOOKUP_DEPTH.bit_length() - 1)
+        rows = lax.broadcasted_iota(jnp.int32, (LOOKUP_DEPTH, LOOKUP_WIDTH), 0)
+        hot = jnp.where(rows == low, 1.0, 0.0).astype(jnp.bfloat16)
+        found = dot_nn(lookup[...], hot)
+        high_rows = jnp.broadcast_to(high_ids, (emb_width, LOOKUP_WIDTH))
+        total = pool_acc[:, columns]
+        picked = jnp.zeros_like(total)
+        for high in range(highs):
+            piece = found[high * emb_width : (high + 1) * emb_width, :]
+            picked = picked + jnp.where(high_rows == high, piece, 0.0)
+        pool_acc[:, columns] = total + picked
+        return carry
+
+    lax.fori_loop(0, steps // 2, look_up, 0)
+    for subset in range(1, 4):
+        gq.forward(subset)
+        go.forward(subset)
+    lax.fori_loop(steps // 2, steps, look_up, 0)
+    for k in range(n_cand):
+        pool_send[k * emb_width : (k + 1) * emb_width, :] = pool_acc[
+            :, k * cand_count : (k + 1) * cand_count
+        ].astype(jnp.bfloat16)
+    pool = (pool_send, pool_recv, pool_sends, pool_recvs, emb_width)
+    start_all(*pool)
+    own_rows(pool_send, pool_recv, emb_width)
+    for subset in range(1, gh.count // 2):
+        gh.forward(subset)
+    for subset in range(4, gq.count // 2):
+        gq.forward(subset)
+        go.forward(subset)
+
+    event = lax.broadcasted_iota(jnp.int32, (events, cand_count), 0)
+    owner = lax.div(lax.rem(event, block_events), shard_events)
+    position = lax.div(event, block_events) * shard_events + lax.rem(event, shard_events)
+    limit = jnp.zeros_like(event)
+    for index in range(owned):
+        limit = jnp.where(owner == index, lens_ref[index], limit)
+    alive = (requests_ref[...] == owner) & (position < limit)
+    live = jnp.where(alive, 1.0, 0.0).T
+
+    wait_all(*pool)
+    pooled = pool_recv[...].astype(jnp.float32).T.astype(jnp.bfloat16)
+    for subset in range(gh.count // 2, gh.count):
+        gh.forward(subset)
+    for subset in range(gq.count // 2, gq.count):
+        gq.forward(subset)
+
+    query_pre = dot_nn(pooled, wq[:pooled_width, :]) + dot_nn(
+        dense_ref[...], wq[pooled_width:, :]
+    )
+    gate = jax.nn.sigmoid(query_pre)
+    query[...] = (query_pre * gate).astype(jnp.bfloat16)
+    slope_pre = gate * (1.0 + query_pre * (1.0 - gate))
+    for head in range(H):
+        cols = slice(head * head_dim, (head + 1) * head_dim)
+        value_cols = slice(model_width + head * head_dim, model_width + (head + 1) * head_dim)
+        scores = dot_nt(query[:, cols], hist[:, cols]) * score_scale
+        chance = jax.nn.sigmoid(scores)
+        weights = (scores * chance * live).astype(jnp.bfloat16)
+        weights_s[head] = weights
+        scores_s[head] = chance * (1.0 + scores * (1.0 - chance)) * live
+        att[:, cols] = dot_nn(weights, hist[:, value_cols])
+    attended = att[...]
+    centered = attended - jnp.mean(attended, axis=1, keepdims=True)
+    inverse = lax.rsqrt(jnp.mean(centered * centered, axis=1, keepdims=True) + norm_eps)
+    normed = centered * inverse
+    for subset in range(go.count // 2, go.count):
+        go.forward(subset)
+    back_y = dot_nt(cot_ref[...], wo[...])
+    back_att[...] = (
+        inverse
+        * (
+            back_y
+            - jnp.mean(back_y, axis=1, keepdims=True)
+            - normed * jnp.mean(back_y * normed, axis=1, keepdims=True)
+        )
+    ).astype(jnp.bfloat16)
+    for head in range(H):
+        cols = slice(head * head_dim, (head + 1) * head_dim)
+        value_cols = slice(model_width + head * head_dim, model_width + (head + 1) * head_dim)
+        back_w = dot_nt(back_att[:, cols], hist[:, value_cols])
+        back_s = (back_w * scores_s[head] * score_scale).astype(jnp.bfloat16)
+        back_query[:, cols] = dot_nn(back_s, hist[:, cols])
+        part[:, cols] = dot_tn(back_s, query[:, cols]).astype(jnp.bfloat16)
+        part[:, value_cols] = dot_tn(weights_s[head], back_att[:, cols]).astype(jnp.bfloat16)
+    parts = (part, part_recv, part_sends, part_recvs, block_events)
+    start_all(*parts)
+    own_rows(part, part_recv, block_events)
+    back_pre = (back_query[...] * slope_pre).astype(jnp.bfloat16)
+    back_columns = dot_nt(wq[:pooled_width, :], back_pre)
+    direct = cot_ref[:, :pooled_width].astype(jnp.float32).T
+    grad_send[...] = (direct + back_columns).astype(jnp.bfloat16)
+    grads = (grad_send, grad_recv, grad_sends, grad_recvs, emb_width)
+    start_all(*grads)
+    own_rows(grad_send, grad_recv, emb_width)
+
+    normed_b = normed.astype(jnp.bfloat16)
+    mixed = dot_nn(normed_b, wo[...])
+    out_ref[:, :pooled_width] = (mixed[:, :pooled_width] + pooled.astype(jnp.float32)).astype(
+        jnp.bfloat16
+    )
+    out_ref[:, pooled_width:] = (
+        mixed[:, pooled_width:] + dense_ref[...].astype(jnp.float32)
+    ).astype(jnp.bfloat16)
+    wait_all(*grads)
+    for k in range(n_cand):
+        dpool_ref[:, k * cand_count : (k + 1) * cand_count] = grad_recv[
+            k * emb_width : (k + 1) * emb_width, :
+        ]
+    wait_all(*parts)
+    total = part_recv[:block_events, :].astype(jnp.float32)
+    for k in range(1, n_cand):
+        total = total + part_recv[k * block_events : (k + 1) * block_events, :].astype(jnp.float32)
+    dkv_ref[...] = total
+    for gather in (gq, gh, go):
+        gather.drain()
+
+
+def one_kernel(
+    n_req,
+    n_cand,
+    dense_feat,
+    emb_ids,
+    tables,
+    history_kv,
+    hist_len,
+    cand_request,
+    w_query,
+    w_out,
+    cotangent,
+):
+    cand_count, model_width = cotangent.shape
+    owned, shard_events, kv_width = history_kv.shape
+    emb_width, table_rows = tables.shape[1:]
+    group_size = emb_ids.shape[2]
+    block_events = owned * shard_events
+    events = block_events * n_cand
+    pooled_width = emb_width * n_cand
+    bf16, f32 = jnp.bfloat16, jnp.float32
+    dma = pltpu.SemaphoreType.DMA
+    vmem = pl.BlockSpec(memory_space=pltpu.VMEM)
+    scratch = [
+        pltpu.VMEM((model_width, model_width), bf16),
+        pltpu.VMEM((model_width, model_width), bf16),
+        pltpu.VMEM((events, kv_width), bf16),
+        pltpu.VMEM((table_rows // LOOKUP_DEPTH * emb_width, LOOKUP_DEPTH), bf16),
+        pltpu.VMEM((emb_width, group_size), f32),
+        pltpu.VMEM((pooled_width, cand_count), bf16),
+        pltpu.VMEM((pooled_width, cand_count), bf16),
+        pltpu.VMEM((cand_count, model_width), f32),
+        pltpu.VMEM((cand_count, model_width), bf16),
+        pltpu.VMEM((cand_count, model_width), bf16),
+        pltpu.VMEM((H, cand_count, events), f32),
+        pltpu.VMEM((H, cand_count, events), bf16),
+        pltpu.VMEM((cand_count, model_width), f32),
+        pltpu.VMEM((events, kv_width), bf16),
+        pltpu.VMEM((events, kv_width), bf16),
+        pltpu.VMEM((pooled_width, cand_count), bf16),
+        pltpu.VMEM((pooled_width, cand_count), bf16),
+    ]
+    scratch += [dma((n_req * n_cand,))] * 4 + [dma((n_cand,))] * 8
+    out, d_kv, d_pooled = pl.pallas_call(
+        functools.partial(layer_kernel, n_req, n_cand),
+        out_shape=(
+            jax.ShapeDtypeStruct((cand_count, model_width), bf16),
+            jax.ShapeDtypeStruct((block_events, kv_width), f32),
+            jax.ShapeDtypeStruct((emb_width, group_size), bf16),
+        ),
+        in_specs=[pl.BlockSpec(memory_space=pltpu.SMEM)] + [vmem] * 8,
+        out_specs=(vmem, vmem, vmem),
+        scratch_shapes=scratch,
+        compiler_params=pltpu.CompilerParams(
+            collective_id=0, has_side_effects=True, vmem_limit_bytes=44 << 20
+        ),
+    )(
+        hist_len,
+        dense_feat,
+        emb_ids.reshape(emb_ids.shape[1:]),
+        tables.reshape(emb_width, table_rows),
+        history_kv.reshape(block_events, kv_width),
+        cand_request.reshape(1, cand_count),
+        w_query,
+        w_out,
+        cotangent,
+    )
+    return (
+        out,
+        d_kv.reshape(history_kv.shape),
+        d_pooled.reshape(1, emb_width, group_size),
+    )
+
+
+def pick_plan(n_req, n_cand, *args):
+    _, emb_ids, tables, history_kv, _, _, w_query, _, _ = args
+    aligned = (
+        tables.shape[0] == 1
+        and w_query.shape[0] % 16 == 0
+        and history_kv.shape[1] % 8 == 0
+        and history_kv.shape[0] * history_kv.shape[1] % 16 == 0
+        and tables.shape[2] % LOOKUP_DEPTH == 0
+        and emb_ids.shape[2] % LOOKUP_WIDTH == 0
+    )
+    if aligned:
+        return one_kernel(n_req, n_cand, *args)
+    return on_device(*args)
+
+
 def solution(mesh):
+    plan = functools.partial(pick_plan, mesh.shape["req"], mesh.shape["cand"])
     return jax.shard_map(
-        on_device,
+        plan,
         mesh=mesh,
         in_specs=(
             P(("req", "cand"), None),

time: 176 us -> 56.4 us (0.32)
  waiting for transfers between devices: 67.7 us -> 0 us
  local copies, waits for them, and re-layouts: 62.1 us -> 8.98 us
  Pallas kernels: 0 us -> 46.3 us
  between operations: 14.2 us -> 0.67 us
  matrix products: 10.6 us -> 0 us
  blocking collectives: 10.3 us -> 0 us
  starting transfers between devices: 8.95 us -> 0 us
    gather x12 -> x0, local copies, waits for them, and re-layouts: 48.2 us -> none  [take_columns(): return jnp.take(table, indices, axis=1)]
    pallas_call x0 -> x1, Pallas kernels: none -> 46.3 us  [one_kernel(): pl.pallas_call(functools.partial(layer_kernel, n_req, n_cand), out_shape=...]
    all_gather x2 -> x0, waiting for transfers between devices: 42 us -> none  [the longest x1 42 us: on_device(): lax.all_gather(w_out, ('req', 'cand'), axis=0, tiled=True)]
    unnamed x4 -> x0, waiting for transfers between devices: 22.2 us -> none
    dot_general x10 -> x0, matrix products: 10.6 us -> none  [the longest x1 2.83 us: on_device(): jnp.dot(features, full_query, preferred_element_type=jnp.float32)]
    all_gather x1 -> x0, blocking collectives: 10.3 us -> none  [on_device(): full_history = lax.all_gather(history_kv, 'cand', axis=1, tiled=True)]
    all_to_all x2 -> x0, starting transfers between devices: 8.84 us -> none  [the longest x1 5.5 us: on_device(): lax.all_to_all(pooled_rows, 'cand', split_axis=1, concat_axis=0, tiled=True)]
    all_to_all x2 -> x0, waiting for transfers between devices: 3.55 us -> none  [the longest x1 3.55 us: on_device(): lax.all_to_all(pool_cols, 'cand', split_axis=0, concat_axis=1, tiled=True)]
  transfers between devices with their start and end apart: 5 -> 0, of which waited for: 3 -> 0; matrix products, arithmetic and copies ran while one was open for 38% -> 0% of each run, Pallas kernels for 0% -> 0%
where the time goes in v1:
time: 56.4 us; the launch traced here: 56 us
  Pallas kernels  46.3 us (82%)
  local copies, waits for them, and re-layouts  8.98 us (16%)
  between operations  0.67 us (1%)
    pallas_call x1, Pallas kernels, one_kernel(): pl.pallas_call(functools.partial(layer_kernel, n_req, n_cand), out_shape=...  46.3 us
    unnamed x21, local copies, waits for them, and re-layouts  8.98 us

profile of v1, /device:TPU:0, one launch (start us, length us, event | category | flops | bytes accessed | tf_op | source)
XLA Modules:
  0.0 56.0 jit_solution(2689524765107450305)
XLA Ops:
  0.6 0.0 copy-start.7
  0.6 0.0 copy-start.8
  0.7 0.6 %copy-done.7 = s32[2]{0:T(128)S(1)} copy-done((s32[2]{0:T(128)S(1)}, s32[2]{0:T(128)}, u32[]{:S(2)}) %copy-start.7) | copy-done | bytes 32
  1.3 0.0 copy-done.8
  1.3 0.0 copy-start
  1.3 1.2 %copy-done = bf16[1,16,32768]{2,1,0:T(8,128)(2,1)S(1)} copy-done((bf16[1,16,32768]{2,1,0:T(8,128)(2,1)S(1)}, bf16[1,16,32768]{2,1,0:T(8,128)(2,1)}, u32[]{:S(2)}) %copy-start) | copy-done | bytes 1048600
  2.5 0.0 copy-start.1
  2.5 0.9 %copy-done.1 = bf16[128,1024]{1,0:T(8,128)(2,1)S(1)} copy-done((bf16[128,1024]{1,0:T(8,128)(2,1)S(1)}, bf16[128,1024]{1,0:T(8,128)(2,1)}, u32[]{:S(2)}) %copy-start.1) | copy-done | bytes 262168
  3.5 0.0 copy-start.2
  3.5 0.9 %copy-done.2 = bf16[128,896]{1,0:T(8,128)(2,1)S(1)} copy-done((bf16[128,896]{1,0:T(8,128)(2,1)S(1)}, bf16[128,896]{1,0:T(8,128)(2,1)}, u32[]{:S(2)}) %copy-start.2) | copy-done | bytes 229400
  4.4 0.0 copy-start.3
  4.4 0.8 %copy-done.3 = bf16[2,8,2048]{2,1,0:T(8,128)(2,1)S(1)} copy-done((bf16[2,8,2048]{2,1,0:T(8,128)(2,1)S(1)}, bf16[2,8,2048]{2,1,0:T(8,128)(2,1)}, u32[]{:S(2)}) %copy-start.3) | copy-done | bytes 65560
  5.3 0.0 copy-start.4
  5.3 0.8 %copy-done.4 = bf16[32,1024]{1,0:T(8,128)(2,1)S(1)} copy-done((bf16[32,1024]{1,0:T(8,128)(2,1)S(1)}, bf16[32,1024]{1,0:T(8,128)(2,1)}, u32[]{:S(2)}) %copy-start.4) | copy-done | bytes 65560
  6.1 0.0 copy-start.5
  6.1 0.8 %copy-done.5 = bf16[32,1024]{1,0:T(8,128)(2,1)S(1)} copy-done((bf16[32,1024]{1,0:T(8,128)(2,1)S(1)}, bf16[32,1024]{1,0:T(8,128)(2,1)}, u32[]{:S(2)}) %copy-start.5) | copy-done | bytes 65560
  6.9 0.0 copy-start.6
  6.9 0.7 %copy-done.6 = s32[1,4,1024]{2,1,0:T(4,128)S(1)} copy-done((s32[1,4,1024]{2,1,0:T(4,128)S(1)}, s32[1,4,1024]{2,1,0:T(4,128)}, u32[]{:S(2)}) %copy-start.6) | copy-done | bytes 16408
  7.7 46.3 %shard_map.112 = (bf16[128,1024]{1,0:T(8,128)(2,1)S(1)}, f32[16,2048]{1,0:T(8,128)S(1)}, bf16[16,1024]{1,0:T(8,128)(2,1)S(1)}) custom-call(s32[2]{0:T(128)S(1)} %copy-done.7, bf16[128,896]{1,0:T(8,128)(2,1)S(1)} %copy-done.2, s32[4,1024]{1,0:T(4,128)S(1)} %bitcast.10, bf16[16,32768]{1,0:T(8,128)(2,1)S(1)} %bitcast.6, bf16[16,2048]{1,0:T(8,128)(2,1)S(1)} %bitcast.8, ...), custom_call_target="tpu_custom_call" | custom-call | tf_op jit(solution)/shard_map/pallas_call | solution.py:497
  54.0 0.7 %copy.15 = bf16[128,1024]{1,0:T(8,128)(2,1)} copy(bf16[128,1024]{1,0:T(8,128)(2,1)S(1)} %get-tuple-element.12) | data formatting | bytes 524288
  54.7 0.7 %copy.16 = f32[2,8,2048]{2,1,0:T(8,128)} copy(f32[2,8,2048]{2,1,0:T(8,128)S(1)} %bitcast.7) | data formatting | bytes 262144
  55.4 0.6 %copy.17 = bf16[1,16,1024]{2,1,0:T(8,128)(2,1)} copy(bf16[1,16,1024]{2,1,0:T(8,128)(2,1)S(1)} %bitcast.9) | data formatting | bytes 65536
Async XLA Ops:
  0.6 0.7 %copy-start.7 = (s32[2]{0:T(128)S(1)}, s32[2]{0:T(128)}, u32[]{:S(2)}) copy-start(s32[2]{0:T(128)} %lens_ref.1) | copy-start | bytes 28
  0.6 0.7 %copy-start.8 = (s32[128]{0:T(128)S(1)}, s32[128]{0:T(128)}, u32[]{:S(2)}) copy-start(s32[128]{0:T(128)} %param.14) | copy-start | bytes 1540
  1.3 1.2 %copy-start = (bf16[1,16,32768]{2,1,0:T(8,128)(2,1)S(1)}, bf16[1,16,32768]{2,1,0:T(8,128)(2,1)}, u32[]{:S(2)}) copy-start(bf16[1,16,32768]{2,1,0:T(8,128)(2,1)} %param.11) | copy-start | bytes 3145732
  2.5 0.9 %copy-start.1 = (bf16[128,1024]{1,0:T(8,128)(2,1)S(1)}, bf16[128,1024]{1,0:T(8,128)(2,1)}, u32[]{:S(2)}) copy-start(bf16[128,1024]{1,0:T(8,128)(2,1)} %cot_ref.1) | copy-start | bytes 786436
  3.5 0.9 %copy-start.2 = (bf16[128,896]{1,0:T(8,128)(2,1)S(1)}, bf16[128,896]{1,0:T(8,128)(2,1)}, u32[]{:S(2)}) copy-start(bf16[128,896]{1,0:T(8,128)(2,1)} %dense_ref.1) | copy-start | bytes 688132
  4.4 0.8 %copy-start.3 = (bf16[2,8,2048]{2,1,0:T(8,128)(2,1)S(1)}, bf16[2,8,2048]{2,1,0:T(8,128)(2,1)}, u32[]{:S(2)}) copy-start(bf16[2,8,2048]{2,1,0:T(8,128)(2,1)} %param.12) | copy-start | bytes 196612
  5.3 0.8 %copy-start.4 = (bf16[32,1024]{1,0:T(8,128)(2,1)S(1)}, bf16[32,1024]{1,0:T(8,128)(2,1)}, u32[]{:S(2)}) copy-start(bf16[32,1024]{1,0:T(8,128)(2,1)} %wq_ref.1) | copy-start | bytes 196612
  6.1 0.8 %copy-start.5 = (bf16[32,1024]{1,0:T(8,128)(2,1)S(1)}, bf16[32,1024]{1,0:T(8,128)(2,1)}, u32[]{:S(2)}) copy-start(bf16[32,1024]{1,0:T(8,128)(2,1)} %wo_ref.1) | copy-start | bytes 196612
  6.9 0.7 %copy-start.6 = (s32[1,4,1024]{2,1,0:T(4,128)S(1)}, s32[1,4,1024]{2,1,0:T(4,128)}, u32[]{:S(2)}) copy-start(s32[1,4,1024]{2,1,0:T(4,128)} %param.10) | copy-start | bytes 49156

commit v2 on v1

--- a/solution.py
+++ b/solution.py
@@ -148,9 +148,10 @@
 
 
 class Gather:
-    def __init__(self, full, own, rounds, place, sends, recvs):
+    def __init__(self, full, own, rounds, place, sends, recvs, first=0):
         self.full, self.own, self.rounds, self.place = full, own, rounds, place
         self.sends, self.recvs, self.rows = sends, recvs, own.shape[0]
+        self.first = first
         self.count = 1 << len(rounds)
 
     def device(self, subset):
@@ -174,8 +175,8 @@
         return pltpu.make_async_remote_copy(
             src_ref=self.own if sent == 0 and not arrived else here,
             dst_ref=here,
-            send_sem=self.sends.at[subset],
-            recv_sem=self.recvs.at[subset],
+            send_sem=self.sends.at[self.first + subset],
+            recv_sem=self.recvs.at[self.first + subset],
             device_id=self.device(1 << step),
             device_id_type=MESH,
         )
@@ -186,8 +187,8 @@
         for step in range(subset.bit_length(), len(self.rounds)):
             self.copy(subset + (1 << step), False).start()
 
-    def keep_own(self):
-        self.block(0)[...] = self.own[...]
+    def keep_own(self, sem):
+        return pltpu.make_async_copy(self.own, self.block(0), sem)
 
     def drain(self):
         for subset in range(1, self.count):
@@ -213,18 +214,24 @@
 def layer_kernel(
     n_req,
     n_cand,
+    lens_hbm,
+    dense_hbm,
+    ids_hbm,
+    table_hbm,
+    hist_ref,
+    requests_hbm,
+    wq_ref,
+    wo_ref,
+    cot_hbm,
+    out_ref,
+    dkv_ref,
+    dpool_ref,
     lens_ref,
     dense_ref,
     ids_ref,
     table_ref,
-    hist_ref,
     requests_ref,
-    wq_ref,
-    wo_ref,
     cot_ref,
-    out_ref,
-    dkv_ref,
-    dpool_ref,
     wq,
     wo,
     hist,
@@ -254,17 +261,34 @@
     part_recvs,
     grad_sends,
     grad_recvs,
+    load_sems,
 ):
     req, cand = lax.axis_index("req"), lax.axis_index("cand")
     cand_count, model_width = cot_ref.shape
     emb_width = table_ref.shape[0]
     head_dim = model_width // H
-    owned = lens_ref.shape[0]
+    owned = lens_ref.shape[1]
     block_events = hist_ref.shape[0]
     events = block_events * n_cand
     shard_events = block_events // owned
     pooled_width = emb_width * n_cand
     score_scale = 1.0 / math.sqrt(head_dim)
+
+    loads = [
+        pltpu.make_async_copy(source, target, load_sems.at[index])
+        for index, (source, target) in enumerate(
+            [
+                (table_hbm, table_ref),
+                (ids_hbm, ids_ref),
+                (lens_hbm, lens_ref),
+                (requests_hbm, requests_ref),
+                (dense_hbm, dense_ref),
+                (cot_hbm, cot_ref),
+            ]
+        )
+    ]
+    for load in loads:
+        load.start()
 
     barrier = pltpu.get_barrier_semaphore()
     greeted = [(flip(req, bit), cand) for bit in powers(n_req)]
@@ -277,20 +301,46 @@
     cand_rounds = [("cand", bit) for bit in powers(n_cand)]
     swapped = cand_rounds[:-1][::-1] + cand_rounds[-1:]
 
-    def linear(r, c):
-        return r * n_cand + c
-
     def in_group(r, c):
         return c
 
-    gq = Gather(wq, wq_ref, req_rounds + cand_rounds, linear, wq_sends, wq_recvs)
-    go = Gather(wo, wo_ref, req_rounds + swapped, linear, wo_sends, wo_recvs)
+    def halves(full, own, sends, recvs):
+        rows = own.shape[0] // 2
+        gathers = []
+        for half, order in enumerate((cand_rounds, swapped)):
+            gathers.append(
+                Gather(
+                    full,
+                    own.at[pl.ds(half * rows, rows)],
+                    req_rounds + order,
+                    lambda r, c, half=half: (r * n_cand + c) * 2 + half,
+                    sends,
+                    recvs,
+                    half * n_req * n_cand,
+                )
+            )
+        return gathers
+
+    gq = halves(wq, wq_ref, wq_sends, wq_recvs)
+    go = halves(wo, wo_ref, wo_sends, wo_recvs)
     gh = Gather(hist, hist_ref, cand_rounds, in_group, hist_sends, hist_recvs)
-    gq.forward(0)
+    last = len(req_rounds + cand_rounds) - 1
+
+    def advance(pair, step):
+        for subset in range((1 << step) // 2, 1 << step):
+            for gather in pair:
+                gather.forward(subset)
+
+    advance(gq, 0)
     gh.forward(0)
-    go.forward(0)
-    for gather in (gq, gh, go):
-        gather.keep_own()
+    loads += [
+        gather.keep_own(load_sems.at[len(loads) + index])
+        for index, gather in enumerate((*gq, gh, *go))
+    ]
+    for load in loads[-5:]:
+        load.start()
+    for load in loads[:2]:
+        load.wait()
 
     def exchange(source, target, sends, recvs, rows, k):
         peer = lax.rem(cand + k, n_cand)
@@ -346,11 +396,12 @@
         pool_acc[:, columns] = total + picked
         return carry
 
-    lax.fori_loop(0, steps // 2, look_up, 0)
-    for subset in range(1, 4):
-        gq.forward(subset)
-        go.forward(subset)
-    lax.fori_loop(steps // 2, steps, look_up, 0)
+    quarter = steps // 4
+    for turn in range(4):
+        lax.fori_loop(turn * quarter, (turn + 1) * quarter, look_up, 0)
+        if turn + 1 < min(4, last):
+            advance(gq, turn + 1)
+            advance(go, turn)
     for k in range(n_cand):
         pool_send[k * emb_width : (k + 1) * emb_width, :] = pool_acc[
             :, k * cand_count : (k + 1) * cand_count
@@ -360,16 +411,18 @@
     own_rows(pool_send, pool_recv, emb_width)
     for subset in range(1, gh.count // 2):
         gh.forward(subset)
-    for subset in range(4, gq.count // 2):
-        gq.forward(subset)
-        go.forward(subset)
-
+    for step in range(min(4, last), last + 1):
+        advance(gq, step)
+        advance(go, step - 1)
+
+    for load in loads[2:]:
+        load.wait()
     event = lax.broadcasted_iota(jnp.int32, (events, cand_count), 0)
     owner = lax.div(lax.rem(event, block_events), shard_events)
     position = lax.div(event, block_events) * shard_events + lax.rem(event, shard_events)
     limit = jnp.zeros_like(event)
     for index in range(owned):
-        limit = jnp.where(owner == index, lens_ref[index], limit)
+        limit = jnp.where(owner == index, lens_ref[:, index : index + 1], limit)
     alive = (requests_ref[...] == owner) & (position < limit)
     live = jnp.where(alive, 1.0, 0.0).T
 
@@ -377,14 +430,14 @@
     pooled = pool_recv[...].astype(jnp.float32).T.astype(jnp.bfloat16)
     for subset in range(gh.count // 2, gh.count):
         gh.forward(subset)
-    for subset in range(gq.count // 2, gq.count):
-        gq.forward(subset)
+    advance(gq, last + 1)
 
     query_pre = dot_nn(pooled, wq[:pooled_width, :]) + dot_nn(
         dense_ref[...], wq[pooled_width:, :]
     )
     gate = jax.nn.sigmoid(query_pre)
     query[...] = (query_pre * gate).astype(jnp.bfloat16)
+    advance(go, last)
     slope_pre = gate * (1.0 + query_pre * (1.0 - gate))
     for head in range(H):
         cols = slice(head * head_dim, (head + 1) * head_dim)
@@ -399,8 +452,7 @@
     centered = attended - jnp.mean(attended, axis=1, keepdims=True)
     inverse = lax.rsqrt(jnp.mean(centered * centered, axis=1, keepdims=True) + norm_eps)
     normed = centered * inverse
-    for subset in range(go.count // 2, go.count):
-        go.forward(subset)
+    advance(go, last + 1)
     back_y = dot_nt(cot_ref[...], wo[...])
     back_att[...] = (
         inverse
@@ -442,13 +494,13 @@
         dpool_ref[:, k * cand_count : (k + 1) * cand_count] = grad_recv[
             k * emb_width : (k + 1) * emb_width, :
         ]
+    for gather in (*gq, gh, *go):
+        gather.drain()
     wait_all(*parts)
     total = part_recv[:block_events, :].astype(jnp.float32)
     for k in range(1, n_cand):
         total = total + part_recv[k * block_events : (k + 1) * block_events, :].astype(jnp.float32)
     dkv_ref[...] = total
-    for gather in (gq, gh, go):
-        gather.drain()
 
 
 def one_kernel(
@@ -474,7 +526,15 @@
     bf16, f32 = jnp.bfloat16, jnp.float32
     dma = pltpu.SemaphoreType.DMA
     vmem = pl.BlockSpec(memory_space=pltpu.VMEM)
-    scratch = [
+    vmem_like = [
+        pltpu.VMEM((1, owned), jnp.int32),
+        pltpu.VMEM((cand_count, model_width - pooled_width), bf16),
+        pltpu.VMEM(emb_ids.shape[1:], jnp.int32),
+        pltpu.VMEM((emb_width, table_rows), bf16),
+        pltpu.VMEM((1, cand_count), jnp.int32),
+        pltpu.VMEM((cand_count, model_width), bf16),
+    ]
+    scratch = vmem_like + [
         pltpu.VMEM((model_width, model_width), bf16),
         pltpu.VMEM((model_width, model_width), bf16),
         pltpu.VMEM((events, kv_width), bf16),
@@ -493,7 +553,7 @@
         pltpu.VMEM((pooled_width, cand_count), bf16),
         pltpu.VMEM((pooled_width, cand_count), bf16),
     ]
-    scratch += [dma((n_req * n_cand,))] * 4 + [dma((n_cand,))] * 8
+    scratch += [dma((2 * n_req * n_cand,))] * 4 + [dma((n_cand,))] * 8 + [dma((11,))]
     out, d_kv, d_pooled = pl.pallas_call(
         functools.partial(layer_kernel, n_req, n_cand),
         out_shape=(
@@ -501,14 +561,14 @@
             jax.ShapeDtypeStruct((block_events, kv_width), f32),
             jax.ShapeDtypeStruct((emb_width, group_size), bf16),
         ),
-        in_specs=[pl.BlockSpec(memory_space=pltpu.SMEM)] + [vmem] * 8,
+        in_specs=[pl.BlockSpec(memory_space=pltpu.HBM)] * 9,
         out_specs=(vmem, vmem, vmem),
         scratch_shapes=scratch,
         compiler_params=pltpu.CompilerParams(
-            collective_id=0, has_side_effects=True, vmem_limit_bytes=44 << 20
+            collective_id=0, has_side_effects=True, vmem_limit_bytes=63 << 20
         ),
     )(
-        hist_len,
+        hist_len.reshape(1, owned),
         dense_feat,
         emb_ids.reshape(emb_ids.shape[1:]),
         tables.reshape(emb_width, table_rows),
@@ -529,10 +589,11 @@
     _, emb_ids, tables, history_kv, _, _, w_query, _, _ = args
     aligned = (
         tables.shape[0] == 1
-        and w_query.shape[0] % 16 == 0
+        and w_query.shape[0] % 32 == 0
         and history_kv.shape[1] % 8 == 0
         and history_kv.shape[0] * history_kv.shape[1] % 16 == 0
         and tables.shape[2] % LOOKUP_DEPTH == 0
+        and emb_ids.shape[1] * emb_ids.shape[2] % (4 * LOOKUP_WIDTH) == 0
         and emb_ids.shape[2] % LOOKUP_WIDTH == 0
     )
     if aligned:

time: 56.4 us -> 49.1 us (0.87)
  local copies, waits for them, and re-layouts: 8.98 us -> 3.08 us
  Pallas kernels: 46.3 us -> 45.2 us
    unnamed x21 -> x7, local copies, waits for them, and re-layouts: 8.98 us -> 3.08 us
    pallas_call x1, Pallas kernels: 46.3 us -> 45.2 us  [one_kernel(): pl.pallas_call(functools.partial(layer_kernel, n_req, n_cand), out_shape=...]
where the time goes in v2:
time: 49.1 us; the launch traced here: 48.9 us
  Pallas kernels  45.2 us (92%)
  local copies, waits for them, and re-layouts  3.08 us (6%)
  between operations  0.65 us (1%)
    pallas_call x1, Pallas kernels, one_kernel(): pl.pallas_call(functools.partial(layer_kernel, n_req, n_cand), out_shape=...  45.2 us
    unnamed x7, local copies, waits for them, and re-layouts  3.08 us

profile of v2, /device:TPU:0, one launch (start us, length us, event | category | flops | bytes accessed | tf_op | source)
XLA Modules:
  0.0 48.9 jit_solution(14054627467900021613)
XLA Ops:
  0.6 45.2 %shard_map.112 = (bf16[128,1024]{1,0:T(8,128)(2,1)}, f32[16,2048]{1,0:T(8,128)}, bf16[16,1024]{1,0:T(8,128)(2,1)}) custom-call(s32[1,2]{1,0:T(1,128)} %bitcast.12, bf16[128,896]{1,0:T(8,128)(2,1)} %dense_hbm.1, s32[4,1024]{1,0:T(4,128)} %bitcast.11, bf16[16,32768]{1,0:T(8,128)(2,1)} %bitcast.7, bf16[16,2048]{1,0:T(8,128)(2,1)} %bitcast.9, ...), custom_call_target="tpu_custom_call" | custom-call | tf_op jit(solution)/shard_map/pallas_call | solution.py:557
  45.8 0.0 copy-start
  45.9 1.7 %copy.15 = bf16[128,1024]{1,0:T(8,128)(2,1)} copy(bf16[128,1024]{1,0:T(8,128)(2,1)} %get-tuple-element.12) | data formatting | bytes 524288
  47.6 0.0 copy-done
  47.6 0.0 copy-start.1
  47.6 0.7 %copy.16 = f32[2,8,2048]{2,1,0:T(8,128)} copy(f32[2,8,2048]{2,1,0:T(8,128)S(1)} %bitcast.8) | data formatting | bytes 262144
  48.2 0.1 copy-done.1
  48.3 0.6 %copy.17 = bf16[1,16,1024]{2,1,0:T(8,128)(2,1)} copy(bf16[1,16,1024]{2,1,0:T(8,128)(2,1)S(1)} %bitcast.10) | data formatting | bytes 65536
Async XLA Ops:
  45.8 1.7 %copy-start = (f32[16,2048]{1,0:T(8,128)S(1)}, f32[16,2048]{1,0:T(8,128)}, u32[]{:S(2)}) copy-start(f32[16,2048]{1,0:T(8,128)} %get-tuple-element.7) | copy-start | bytes 393220
  47.6 0.8 %copy-start.1 = (bf16[16,1024]{1,0:T(8,128)(2,1)S(1)}, bf16[16,1024]{1,0:T(8,128)(2,1)}, u32[]{:S(2)}) copy-start(bf16[16,1024]{1,0:T(8,128)(2,1)} %get-tuple-element.8) | copy-start | bytes 98308

commit v3 on v2

--- a/solution.py
+++ b/solution.py
@@ -304,7 +304,7 @@
     def in_group(r, c):
         return c
 
-    def halves(full, own, sends, recvs):
+    def halves(full, own, sends, recvs, ahead):
         rows = own.shape[0] // 2
         gathers = []
         for half, order in enumerate((cand_rounds, swapped)):
@@ -312,7 +312,7 @@
                 Gather(
                     full,
                     own.at[pl.ds(half * rows, rows)],
-                    req_rounds + order,
+                    order[:ahead] + req_rounds + order[ahead:],
                     lambda r, c, half=half: (r * n_cand + c) * 2 + half,
                     sends,
                     recvs,
@@ -321,8 +321,8 @@
             )
         return gathers
 
-    gq = halves(wq, wq_ref, wq_sends, wq_recvs)
-    go = halves(wo, wo_ref, wo_sends, wo_recvs)
+    gq = halves(wq, wq_ref, wq_sends, wq_recvs, 0)
+    go = halves(wo, wo_ref, wo_sends, wo_recvs, 1)
     gh = Gather(hist, hist_ref, cand_rounds, in_group, hist_sends, hist_recvs)
     last = len(req_rounds + cand_rounds) - 1
 

time: 49.1 us -> 48.1 us (0.980)
  Pallas kernels: 45.2 us -> 44.1 us
    pallas_call x1, Pallas kernels: 45.2 us -> 44.1 us  [one_kernel(): pl.pallas_call(functools.partial(layer_kernel, n_req, n_cand), out_shape=...]
where the time goes in v3:
time: 48.1 us; the launch traced here: 47.9 us
  Pallas kernels  44.1 us (92%)
  local copies, waits for them, and re-layouts  3.08 us (6%)
  between operations  0.65 us (1%)
    pallas_call x1, Pallas kernels, one_kernel(): pl.pallas_call(functools.partial(layer_kernel, n_req, n_cand), out_shape=...  44.1 us
    unnamed x7, local copies, waits for them, and re-layouts  3.08 us

profile of v3, /device:TPU:0, one launch (start us, length us, event | category | flops | bytes accessed | tf_op | source)
XLA Modules:
  0.0 47.9 jit_solution(17863347460852683121)
XLA Ops:
  0.6 44.1 %shard_map.112 = (bf16[128,1024]{1,0:T(8,128)(2,1)}, f32[16,2048]{1,0:T(8,128)}, bf16[16,1024]{1,0:T(8,128)(2,1)}) custom-call(s32[1,2]{1,0:T(1,128)} %bitcast.12, bf16[128,896]{1,0:T(8,128)(2,1)} %dense_hbm.1, s32[4,1024]{1,0:T(4,128)} %bitcast.11, bf16[16,32768]{1,0:T(8,128)(2,1)} %bitcast.7, bf16[16,2048]{1,0:T(8,128)(2,1)} %bitcast.9, ...), custom_call_target="tpu_custom_call" | custom-call | tf_op jit(solution)/shard_map/pallas_call | solution.py:557
  44.8 0.0 copy-start
  44.8 1.7 %copy.15 = bf16[128,1024]{1,0:T(8,128)(2,1)} copy(bf16[128,1024]{1,0:T(8,128)(2,1)} %get-tuple-element.12) | data formatting | bytes 524288
  46.5 0.0 copy-done
  46.5 0.0 copy-start.1
  46.5 0.7 %copy.16 = f32[2,8,2048]{2,1,0:T(8,128)} copy(f32[2,8,2048]{2,1,0:T(8,128)S(1)} %bitcast.8) | data formatting | bytes 262144
  47.1 0.1 copy-done.1
  47.2 0.6 %copy.17 = bf16[1,16,1024]{2,1,0:T(8,128)(2,1)} copy(bf16[1,16,1024]{2,1,0:T(8,128)(2,1)S(1)} %bitcast.10) | data formatting | bytes 65536
Async XLA Ops:
  44.8 1.7 %copy-start = (f32[16,2048]{1,0:T(8,128)S(1)}, f32[16,2048]{1,0:T(8,128)}, u32[]{:S(2)}) copy-start(f32[16,2048]{1,0:T(8,128)} %get-tuple-element.7) | copy-start | bytes 393220
  46.5 0.8 %copy-start.1 = (bf16[16,1024]{1,0:T(8,128)(2,1)S(1)}, bf16[16,1024]{1,0:T(8,128)(2,1)}, u32[]{:S(2)}) copy-start(bf16[16,1024]{1,0:T(8,128)(2,1)} %get-tuple-element.8) | copy-start | bytes 98308
